TPU v7x, 32 devices: a whole 2x2x4 slice. The times are simulated.
32 devices in a mesh: parts: 2 (over y), row: 4 (over z), col: 2 (over x), sub: 2 (over core).
Axes of the slice: x: 2, y: 2, z: 4, core: 2. Of those that a mesh axis runs over, the one named last changes fastest.
Arguments:
- tiles: float32 [128, 256, 256], P(('parts', 'row', 'col')), parts along dimension 0, may hold values from 0.01 to 1
- tile_rows: int32 [128], P(('parts', 'row', 'col')), parts along dimension 0, may hold values from 0 to 1, as said below
- tile_cols: int32 [128], P(('parts', 'row', 'col')), parts along dimension 0, may hold values from 0 to 3
- tile_counts: int32 [16], P(('parts', 'row', 'col')), parts along dimension 0, may hold values from 2 to 8
- start_panel: float32 [4096, 32], P(('parts', 'row', 'col'), 'sub'), parts along dimension 0, may hold values from -6 to 6
Outputs:
- lanczos_panel: float32 [4096, 32], P(('parts', 'row', 'col'), 'sub'), parts along dimension 0
- alphas: float32 [6, 32, 32], P('parts'), parts along dimension 0
- betas: float32 [8, 32, 32], P('parts'), parts along dimension 0
There are 2 independent parts, one for each index of `parts`. A program takes and returns all parts, laid end to end along the dimension named above; each array names one. Nothing has to cross between parts.
Inputs may be any that keep to these rules, and one draw needn't show every extreme that they name: `tile_rows`: within one index pair of row and col, slots hold distinct pairs of row and column block.
All inputs are finite; a program needn't handle non-finite values.
Results may differ from a plain program's by a relative error of at most 0.0003.
Values sent between devices are 32-bit elements; how exact they have to be, the bound alone decides.
A program may use at most 64 MiB of HBM per device.

v0:
```python
import jax
import jax.numpy as jnp
from jax import lax
from jax.sharding import PartitionSpec as P

ITERS = 3


def full_dot(left, right):
    return jnp.dot(left, right, precision=lax.Precision.HIGHEST)


def join_halves(half):
    return lax.all_gather(half, "sub", axis=1, tiled=True)


def factorize(gram_matrix, panel):
    factor = jnp.linalg.cholesky(gram_matrix)
    result = jax.scipy.linalg.solve_triangular(factor, panel.T, lower=True).T
    return (result, factor)


def tile_products(
    pooled_tiles, pooled_rows, pooled_cols, slot_of, first_index, end_index, blocks, row_total
):
    tile_side = pooled_tiles.shape[1]
    half_width = blocks.shape[2]
    per_turn = 4
    turn_count = (end_index - first_index + per_turn - 1) // per_turn

    def one_turn(position, summed):
        virtual = first_index + position * per_turn + jnp.arange(per_turn, dtype=jnp.int32)
        active = virtual < end_index
        clamped = jnp.clip(slot_of(virtual), 0, pooled_tiles.shape[0] - 1)
        chosen = jnp.take(pooled_tiles, clamped, axis=0)
        needed = jnp.take(blocks, jnp.take(pooled_cols, clamped), axis=0)
        product = jnp.einsum("gab,gbc->gac", chosen, needed, precision=lax.Precision.HIGHEST)
        targets = jnp.take(pooled_rows, clamped)
        select = (
            (targets[:, None] == jnp.arange(row_total, dtype=jnp.int32)[None, :]) & active[:, None]
        ).astype(jnp.float32)
        return summed + jnp.einsum("gr,gac->rac", select, product, precision=lax.Precision.HIGHEST)

    empty = jnp.zeros((row_total, tile_side, half_width), jnp.float32)
    return lax.fori_loop(0, turn_count, one_turn, empty)


def on_device(tiles, tile_rows, tile_cols, tile_counts, start_panel):
    slot_count = tiles.shape[0]
    tile_side = tiles.shape[1]
    local_rows = start_panel.shape[0]
    half_width = start_panel.shape[1]
    local_blocks = local_rows // tile_side
    row_span = local_blocks * lax.axis_size("col")
    my_count = tile_counts[0]
    side = lax.axis_index("sub")
    own_active = jnp.arange(slot_count, dtype=jnp.int32) < my_count
    in_use = own_active.astype(jnp.float32)
    row_sums = jnp.sum(tiles, axis=2)
    placing = (tile_rows[:, None] == jnp.arange(row_span, dtype=jnp.int32)[None, :]).astype(
        jnp.float32
    ) * in_use[:, None]
    partial_degree = full_dot(placing.T, row_sums).reshape(-1)
    degree = 1.0 + lax.psum_scatter(partial_degree, "col", scatter_dimension=0, tiled=True)
    inv_root = (1.0 / jnp.sqrt(degree))[:, None]

    def identity_slot(virtual):
        return virtual

    start_full = join_halves(start_panel)
    start_gram = lax.psum(full_dot(start_full.T, start_full), ("row", "col"))
    current, factor = factorize(start_gram, start_full)
    betas = [factor.T]
    alphas = []
    previous = None
    for iteration in range(ITERS):
        current_half = lax.dynamic_slice_in_dim(current, side * half_width, half_width, 1)
        scaled_half = inv_root * current_half
        gathered = lax.all_gather(scaled_half, "row", axis=0, tiled=True)
        blocks = gathered.reshape(-1, tile_side, half_width)
        summed = tile_products(
            tiles, tile_rows, tile_cols, identity_slot, 0, my_count, blocks, row_span
        )
        partial_value = summed.reshape(row_span * tile_side, half_width)
        new_half = inv_root * lax.psum_scatter(
            partial_value, "col", scatter_dimension=0, tiled=True
        )
        residual = join_halves(new_half)
        if previous is not None:
            residual = residual - full_dot(previous, betas[-1].T)
        alpha_block = lax.psum(full_dot(current.T, residual), ("row", "col"))
        residual = residual - full_dot(current, alpha_block)
        gram_matrix = lax.psum(full_dot(residual.T, residual), ("row", "col"))
        following, factor = factorize(gram_matrix, residual)
        alphas.append(alpha_block)
        betas.append(factor.T)
        previous, current = (current, following)
    final_half = lax.dynamic_slice_in_dim(current, side * half_width, half_width, 1)
    return (final_half, jnp.stack(alphas), jnp.stack(betas))


def solution(mesh):
    return jax.shard_map(
        on_device,
        mesh=mesh,
        in_specs=(
            P(("parts", "row", "col"), None, None),
            P(("parts", "row", "col")),
            P(("parts", "row", "col")),
            P(("parts", "row", "col")),
            P(("parts", "row", "col"), "sub"),
        ),
        out_specs=(
            P(("parts", "row", "col"), "sub"),
            P("parts", None, None),
            P("parts", None, None),
        ),
        check_vma=False,
    )
```

profile of v0, /device:TPU:0, one launch (start us, length us, event | category | flops | bytes accessed | tf_op | source)
XLA Modules:
  0.0 403.5 jit_solution(12598874579051265338)
XLA Ops:
  8.1 1.9 reduce_sum.9
  10.3 5.8 %all-reduce = f32[512]{0:T(512)S(1)} all-reduce(f32[512]{0:T(512)S(1)} %bitcast.159), channel_id=2, replica_groups=mesh['parts'=2,'row'=4,'col'=2,'sub'=2] {'col'}, use_global_device_ids=true, to_apply=%region_1.0.clone | all-reduce | flops 512 | bytes 4096
  16.1 1.8 all_gather.21
  18.1 37.9 %psum.49 = f32[32,32]{0,1:T(8,128)S(1)} all-reduce(f32[32,32]{0,1:T(8,128)S(1)} %fusion.102), channel_id=1, replica_groups=mesh['parts'=2,'row'=4,'col'=2,'sub'=2] {'row','col'}, use_global_device_ids=true, to_apply=%region_2.0 | all-reduce | flops 1024 | bytes 8192 | tf_op jit(solution)/shard_map/psum | solution.py:71
  56.1 2.9 cholesky.74
  59.7 0.7 fusion.81
  60.4 2.4 custom-call.8
  64.4 13.1 %all_gather.22 = f32[1024,16]{0,1:T(8,128)S(1)} all-gather(f32[256,16]{0,1:T(8,128)S(1)} %multiply_bitcast_fusion.2), channel_id=1, replica_groups=mesh['parts'=2,'row'=4,'col'=2,'sub'=2] {'row'}, dimensions={0}, use_global_device_ids=true | all-gather | bytes 81920 | tf_op jit(solution)/shard_map/all_gather | solution.py:79
  77.6 4.6 %while.30 = (s32[]{:T(128)}, f32[2,256,16]{1,0,2:T(2,128)S(1)}, s32[]{:T(128)}, s32[8]{0:T(128)S(1)}, s32[]{:T(128)}, /*index=5*/f32[8,256,256]{2,1,0:T(8,128)S(...) while((s32[]{:T(128)}, f32[2,256,16]{1,0,2:T(2,128)S(1)}, s32[]{:T(128)}, ...), condition=%wide.region_6.12_spmd, body=%wide.region_5.11_spmd.sunk | while | flops 51013772 | bytes 3547549 | solution.py:45
  77.6 0.7 fusion.155
  80.8 1.1 fusion.154
  82.9 11.8 %reduce-scatter.4.cloned.1.call-done = f32[256,16]{0,1:T(8,128)} async-done(((f32[512,16]{0,1:T(8,128)}), f32[256,16]{0,1:T(8,128)}) %reduce-scatter.4.cloned.1.call-update) | async-done | bytes 16400 | tf_op jit(solution)/shard_map/reduce_scatter | solution.py:85
  94.6 0.7 broadcast_multiply_fusion.2
  95.4 1.8 all_gather.23
  97.3 36.2 %psum.50 = f32[32,32]{1,0:T(8,128)S(1)} all-reduce(f32[32,32]{1,0:T(8,128)S(1)} %fusion.103), channel_id=1, replica_groups=mesh['parts'=2,'row'=4,'col'=2,'sub'=2] {'row','col'}, use_global_device_ids=true, to_apply=%region_8.14 | all-reduce | flops 1024 | bytes 8192 | tf_op jit(solution)/shard_map/psum | solution.py:91
  133.9 33.0 %psum.51 = f32[32,32]{0,1:T(8,128)S(1)} all-reduce(f32[32,32]{0,1:T(8,128)S(1)} %fusion.104), channel_id=1, replica_groups=mesh['parts'=2,'row'=4,'col'=2,'sub'=2] {'row','col'}, use_global_device_ids=true, to_apply=%region_9.15 | all-reduce | flops 1024 | bytes 8192 | tf_op jit(solution)/shard_map/psum | solution.py:93
  167.0 2.9 cholesky.85
  169.9 0.7 compare_reduce_fusion.2
  170.6 0.7 fusion.84
  171.3 2.4 custom-call.9
  174.1 13.1 %all_gather.24 = f32[1024,16]{0,1:T(8,128)S(1)} all-gather(f32[256,16]{0,1:T(8,128)S(1)} %multiply_bitcast_fusion.1), channel_id=1, replica_groups=mesh['parts'=2,'row'=4,'col'=2,'sub'=2] {'row'}, dimensions={0}, use_global_device_ids=true | all-gather | bytes 81920 | tf_op jit(solution)/shard_map/all_gather | solution.py:79
  187.2 4.6 %while.31 = (s32[]{:T(128)}, f32[2,256,16]{1,0,2:T(2,128)S(1)}, s32[]{:T(128)}, s32[8]{0:T(128)S(1)}, s32[]{:T(128)}, /*index=5*/f32[8,256,256]{2,1,0:T(8,128)S(...) while((s32[]{:T(128)}, f32[2,256,16]{1,0,2:T(2,128)S(1)}, s32[]{:T(128)}, ...), condition=%wide.region_11.17_spmd, body=%wide.region_10.16_spmd.sunk | while | flops 51013772 | bytes 3547549 | solution.py:45
  187.2 0.7 fusion.161
  190.4 1.1 fusion.160
  192.5 11.7 %reduce-scatter.6.cloned.1.call-done = f32[256,16]{0,1:T(8,128)} async-done(((f32[512,16]{0,1:T(8,128)}), f32[256,16]{0,1:T(8,128)}) %reduce-scatter.6.cloned.1.call-update) | async-done | bytes 16400 | tf_op jit(solution)/shard_map/reduce_scatter | solution.py:85
  204.2 0.7 broadcast_multiply_fusion.1
  205.0 1.8 all_gather.25
  206.8 0.9 convolution_subtract_fusion.3
  207.9 36.2 %psum.52 = f32[32,32]{1,0:T(8,128)S(1)} all-reduce(f32[32,32]{1,0:T(8,128)S(1)} %fusion.105), channel_id=1, replica_groups=mesh['parts'=2,'row'=4,'col'=2,'sub'=2] {'row','col'}, use_global_device_ids=true, to_apply=%region_13.19 | all-reduce | flops 1024 | bytes 8192 | tf_op jit(solution)/shard_map/psum | solution.py:91
  244.4 33.0 %psum.53 = f32[32,32]{0,1:T(8,128)S(1)} all-reduce(f32[32,32]{0,1:T(8,128)S(1)} %fusion.106), channel_id=1, replica_groups=mesh['parts'=2,'row'=4,'col'=2,'sub'=2] {'row','col'}, use_global_device_ids=true, to_apply=%region_14.20 | all-reduce | flops 1024 | bytes 8192 | tf_op jit(solution)/shard_map/psum | solution.py:93
  277.5 2.9 cholesky.96
  280.4 0.7 compare_reduce_fusion.1
  281.2 0.7 fusion.82
  281.9 2.4 custom-call.10
  284.6 13.1 %all_gather.26 = f32[1024,16]{0,1:T(8,128)S(1)} all-gather(f32[256,16]{0,1:T(8,128)S(1)} %multiply_bitcast_fusion), channel_id=1, replica_groups=mesh['parts'=2,'row'=4,'col'=2,'sub'=2] {'row'}, dimensions={0}, use_global_device_ids=true | all-gather | bytes 81920 | tf_op jit(solution)/shard_map/all_gather | solution.py:79
  297.7 4.6 %while.32 = (s32[]{:T(128)}, f32[2,256,16]{1,0,2:T(2,128)S(1)}, s32[]{:T(128)}, s32[8]{0:T(128)S(1)}, s32[]{:T(128)}, /*index=5*/f32[8,256,256]{2,1,0:T(8,128)S(...) while((s32[]{:T(128)}, f32[2,256,16]{1,0,2:T(2,128)S(1)}, s32[]{:T(128)}, ...), condition=%wide.region_16.22_spmd, body=%wide.region_15.21_spmd.sunk | while | flops 51013772 | bytes 3547549 | solution.py:45
  297.7 0.7 fusion.167
  300.9 1.1 fusion.166
  303.0 11.8 %reduce-scatter.8.cloned.1.call-done = f32[256,16]{0,1:T(8,128)} async-done(((f32[512,16]{0,1:T(8,128)}), f32[256,16]{0,1:T(8,128)}) %reduce-scatter.8.cloned.1.call-update) | async-done | bytes 16400 | tf_op jit(solution)/shard_map/reduce_scatter | solution.py:85
  314.8 0.7 broadcast_multiply_fusion
  315.5 1.8 all_gather.27
  317.3 0.9 convolution_subtract_fusion.1
  318.4 36.2 %psum.54 = f32[32,32]{1,0:T(8,128)S(1)} all-reduce(f32[32,32]{1,0:T(8,128)S(1)} %fusion.107), channel_id=1, replica_groups=mesh['parts'=2,'row'=4,'col'=2,'sub'=2] {'row','col'}, use_global_device_ids=true, to_apply=%region_18.24 | all-reduce | flops 1024 | bytes 8192 | tf_op jit(solution)/shard_map/psum | solution.py:91
  354.9 33.0 %psum.55 = f32[32,32]{0,1:T(8,128)S(1)} all-reduce(f32[32,32]{0,1:T(8,128)S(1)} %fusion.108), channel_id=1, replica_groups=mesh['parts'=2,'row'=4,'col'=2,'sub'=2] {'row','col'}, use_global_device_ids=true, to_apply=%region_19.25 | all-reduce | flops 1024 | bytes 8192 | tf_op jit(solution)/shard_map/psum | solution.py:93
  388.0 2.9 cholesky.107
  391.6 0.7 fusion.80
  392.3 0.7 copy.46
  393.0 2.4 custom-call.11
  (94 shorter events, 17.1 us)
Async XLA Ops:
  7.2 55.9 %copy-start.4 = (u32[32]{0:T(128)S(1)}, u32[32]{0:T(128)}, u32[]{:S(2)}) copy-start(u32[32]{0:T(128)} %constant.129) | copy-start | bytes 388
  7.2 70.4 %copy-start.2 = (f32[8,256,256]{2,1,0:T(8,128)S(1)}, f32[8,256,256]{2,1,0:T(8,128)}, u32[]{:S(2)}) copy-start(f32[8,256,256]{2,1,0:T(8,128)} %param.20) | copy-start | bytes 6291460
  7.2 2.8 copy-start
  7.2 8.9 %copy-start.3 = (f32[256,16]{0,1:T(8,128)S(1)}, f32[256,16]{0,1:T(8,128)}, u32[]{:S(2)}) copy-start(f32[256,16]{0,1:T(8,128)} %param.24) | copy-start | bytes 49156
  7.2 70.4 %copy-start.1 = (s32[8]{0:T(128)S(1)}, s32[8]{0:T(128)}, u32[]{:S(2)}) copy-start(s32[8]{0:T(128)} %param.22) | copy-start | bytes 100
  7.2 87.4 %reduce-scatter.4.cloned.1.call-start = ((), (), s32[]{:S(2)}) async-start(), calls=%async_computation.3 | async-start | bytes 49152 | tf_op jit(solution)/shard_map/reduce_scatter | solution.py:85
  82.8 121.4 %reduce-scatter.6.cloned.1.call-start = ((), (), s32[]{:S(2)}) async-start(), calls=%async_computation.4 | async-start | bytes 49152 | tf_op jit(solution)/shard_map/reduce_scatter | solution.py:85
  192.4 122.3 %reduce-scatter.8.cloned.1.call-start = ((), (), s32[]{:S(2)}) async-start(), calls=%async_computation.5 | async-start | bytes 49152 | tf_op jit(solution)/shard_map/reduce_scatter | solution.py:85
Sparse Core Ops, SparseCore 0:
  82.9 11.6 reduce-scatter.3
  192.6 11.6 reduce-scatter.5
  303.1 11.6 reduce-scatter.7
where the time goes:
time: 404 us; the launch traced here: 403 us
  blocking collectives  298 us (74%)
  waiting for transfers between devices  35.3 us (9%)
  other arithmetic  33.9 us (8%)
  between operations  15.5 us (4%)
  local copies, waits for them, and re-layouts  11.5 us (3%)
  matrix products  8.95 us (2%)
    psum x3, blocking collectives, on_device(): alpha_block = lax.psum(full_dot(current.T, residual), ('row', 'col'))  108 us
    psum x3, blocking collectives, on_device(): gram_matrix = lax.psum(full_dot(residual.T, residual), ('row', 'col'))  98.9 us
    all_gather x3, blocking collectives, on_device(): gathered = lax.all_gather(scaled_half, 'row', axis=0, tiled=True)  39.4 us
    psum x1, blocking collectives, on_device(): start_gram = lax.psum(full_dot(start_full.T, start_full), ('row', 'col'))  37.9 us
    reduce_scatter x3, waiting for transfers between devices, on_device(): lax.psum_scatter(partial_value, 'col', scatter_dimension=0, tiled=True)  35.3 us
    another operation x12, other arithmetic, factorize(): factor = jnp.linalg.cholesky(gram_matrix)  14.5 us
    another operation x4, other arithmetic, factorize(): result = jax.scipy.linalg.solve_triangular(factor, panel.T, lower=True).T  9.74 us
  transfers between devices with their start and end apart: 3, of which 3 were waited for; matrix products, arithmetic and copies ran while one was open for 0% of the time, Pallas kernels for 0%

commit v1 on v0

--- a/solution.py
+++ b/solution.py
@@ -1,6 +1,10 @@
+import functools
+
 import jax
 import jax.numpy as jnp
 from jax import lax
+from jax.experimental import pallas as pl
+from jax.experimental.pallas import tpu as pltpu
 from jax.sharding import PartitionSpec as P
 
 ITERS = 3
@@ -99,9 +103,277 @@
     return (final_half, jnp.stack(alphas), jnp.stack(betas))
 
 
+LAST = (((1,), (1,)), ((), ()))
+
+
+def dot_last(left, right):
+    return lax.dot_general(
+        left, right, LAST, precision=lax.Precision.HIGHEST, preferred_element_type=jnp.float32
+    )
+
+
+def split_two(value):
+    high = value.astype(jnp.bfloat16)
+    low = (value - high.astype(jnp.float32)).astype(jnp.bfloat16)
+    return high, low
+
+
+def triangular_parts(gram):
+    width = gram.shape[0]
+    rows = lax.broadcasted_iota(jnp.int32, (width, width), 0)
+    lanes = lax.broadcasted_iota(jnp.int32, (width, width), 1)
+    upper = gram
+    inverse = (rows == lanes).astype(jnp.float32)
+    pivots = []
+    group = 8
+    for first in range(0, width, group):
+        columns = [
+            jnp.broadcast_to(upper[:, at : at + 1], (width, width))
+            for at in range(first, first + group)
+        ]
+        for at in range(first, first + group):
+            column = columns[at - first]
+            pivot = column[at : at + 1, :]
+            pivots.append(pivot)
+            factor = jnp.where(rows > at, column * (1.0 / pivot), 0.0)
+            for later in range(at + 1, first + group):
+                other = columns[later - first]
+                columns[later - first] = other - factor * other[at : at + 1, :]
+            upper = upper - factor * upper[at : at + 1, :]
+            inverse = inverse - factor * inverse[at : at + 1, :]
+    scale = 1.0 / jnp.sqrt(jnp.concatenate(pivots, axis=0))
+    return jnp.where(lanes >= rows, upper * scale, 0.0), inverse * scale
+
+
+def lanczos_kernel(
+    n_row, n_col, n_sub,
+    rows_ref, cols_ref, count_ref, tiles_ref, start_ref,
+    panel_ref, alphas_ref, betas_ref,
+    tiles_buf, tile_high, tile_low, start_buf, sums_buf, part_buf,
+    root_ref, current_ref, previous_ref, residual_ref,
+    tile_sem, start_send, start_recv, sums_send, sums_recv, part_send, part_recv,
+):
+    slots, side, _ = tiles_ref.shape
+    half = side // n_sub
+    local_cols = slots // n_col
+    width = part_buf.shape[2]
+    half_width = width // n_sub
+    devices = n_row * n_col * n_sub
+    row = lax.axis_index("row")
+    col = lax.axis_index("col")
+    sub = lax.axis_index("sub")
+    me = (row * n_col + col) * n_sub + sub
+
+    def place(peer):
+        return {
+            "row": peer // (n_col * n_sub),
+            "col": (peer // n_sub) % n_col,
+            "sub": peer % n_sub,
+        }
+
+    def other(step):
+        return lax.rem(me + step, devices)
+
+    tile_copies = []
+    for slot in range(slots):
+        copy = pltpu.make_async_copy(
+            tiles_ref.at[slot, pl.ds(pl.multiple_of(sub * half, half), half), :],
+            tiles_buf.at[slot],
+            tile_sem.at[slot],
+        )
+        copy.start()
+        tile_copies.append(copy)
+
+    barrier = pltpu.get_barrier_semaphore()
+    for step in range(1, devices):
+        pl.semaphore_signal(
+            barrier, inc=1, device_id=place(other(step)), device_id_type=pl.DeviceIdType.MESH
+        )
+    start_buf[me] = start_ref[...].T
+    pl.semaphore_wait(barrier, devices - 1)
+
+    def copies(buf, send, recv):
+        return [
+            pltpu.make_async_remote_copy(
+                src_ref=buf.at[me],
+                dst_ref=buf.at[me],
+                send_sem=send.at[step],
+                recv_sem=recv.at[me],
+                device_id=place(other(step)),
+                device_id_type=pl.DeviceIdType.MESH,
+            )
+            for step in range(1, devices)
+        ]
+
+    def send_all(buf, send, recv):
+        for copy in copies(buf, send, recv):
+            copy.start()
+
+    def wait_all(buf, send, recv):
+        for step in range(1, devices):
+            peer = other(step)
+            pltpu.make_async_remote_copy(
+                src_ref=buf.at[peer],
+                dst_ref=buf.at[peer],
+                send_sem=send.at[step],
+                recv_sem=recv.at[peer],
+                device_id=place(peer),
+                device_id_type=pl.DeviceIdType.MESH,
+            ).wait_recv()
+
+    def wait_sent(buf, send, recv):
+        for copy in copies(buf, send, recv):
+            copy.wait_send()
+
+    send_all(start_buf, start_send, start_recv)
+
+    for copy in tile_copies:
+        copy.wait()
+    for block in range(n_col):
+        for column in range(local_cols):
+            slot = jnp.int32(0)
+            for candidate in range(slots):
+                here = (rows_ref[candidate] == block) & (cols_ref[candidate] == column)
+                slot = jnp.where(here, candidate, slot)
+            in_use = jnp.where(slot < count_ref[0], 1.0, 0.0)
+            high, low = split_two(tiles_buf[slot] * in_use)
+            at = (slice(block * half, (block + 1) * half), slice(column * side, (column + 1) * side))
+            tile_high[at] = high
+            tile_low[at] = low
+    ones = jnp.ones((8, local_cols * side), jnp.bfloat16)
+    sums_buf[me] = lax.dot_general(
+        ones, tile_high[...], LAST, preferred_element_type=jnp.float32
+    ) + lax.dot_general(ones, tile_low[...], LAST, preferred_element_type=jnp.float32)
+    send_all(sums_buf, sums_send, sums_recv)
+
+    wait_all(start_buf, start_send, start_recv)
+    for block in range(n_row * n_col):
+        for part in range(n_sub):
+            residual_ref[
+                part * half_width : (part + 1) * half_width, block * side : (block + 1) * side
+            ] = start_buf[block * n_sub + part]
+
+    def orthonormalize(at):
+        panel = residual_ref[...]
+        upper, inverse = triangular_parts(dot_last(panel, panel))
+        betas_ref[at] = upper
+        current_ref[...] = full_dot(inverse, panel)
+        return upper
+
+    beta = orthonormalize(0)
+
+    def assemble(buf, target, finish):
+        for r in range(n_row):
+            for s in range(n_sub):
+                total = buf[(r * n_col) * n_sub + s]
+                for c in range(1, n_col):
+                    total = total + buf[(r * n_col + c) * n_sub + s]
+                for block in range(n_col):
+                    first = (r * n_col + block) * side + s * half
+                    target[:, first : first + half] = finish(
+                        total[:, block * half : (block + 1) * half], first
+                    )
+
+    wait_all(sums_buf, sums_send, sums_recv)
+    assemble(sums_buf, root_ref, lambda total, first: 1.0 / jnp.sqrt(1.0 + total))
+
+    for iteration in range(alphas_ref.shape[0]):
+        highs, lows = [], []
+        for column in range(local_cols):
+            at = pl.ds(pl.multiple_of((column * n_col + col) * side, side), side)
+            high, low = split_two(current_ref[:, at] * root_ref[0:1, at])
+            highs.append(high)
+            lows.append(low)
+        high = jnp.concatenate(highs, axis=1)
+        both = jnp.concatenate([high, jnp.concatenate(lows, axis=1)], axis=0)
+        first = lax.dot_general(both, tile_high[...], LAST, preferred_element_type=jnp.float32)
+        second = lax.dot_general(high, tile_low[...], LAST, preferred_element_type=jnp.float32)
+        buf = part_buf.at[iteration]
+        send = part_send.at[iteration]
+        recv = part_recv.at[iteration]
+        buf[me] = first[:width] + (first[width:] + second)
+        send_all(buf, send, recv)
+        wait_all(buf, send, recv)
+        assemble(
+            buf, residual_ref, lambda total, first: total * root_ref[0:1, first : first + half]
+        )
+        residual = residual_ref[...]
+        if iteration > 0:
+            residual = residual - full_dot(beta, previous_ref[...])
+        current = current_ref[...]
+        alpha = dot_last(current, residual)
+        alphas_ref[iteration] = alpha
+        residual_ref[...] = residual - full_dot(alpha.T, current)
+        previous_ref[...] = current
+        beta = orthonormalize(iteration + 1)
+
+    own = pl.ds(pl.multiple_of((row * n_col + col) * side, side), side)
+    rows_own = pl.ds(pl.multiple_of(sub * half_width, half_width), half_width)
+    panel_ref[...] = current_ref[rows_own, own].T
+
+    wait_sent(start_buf, start_send, start_recv)
+    wait_sent(sums_buf, sums_send, sums_recv)
+    for iteration in range(alphas_ref.shape[0]):
+        wait_sent(part_buf.at[iteration], part_send.at[iteration], part_recv.at[iteration])
+
+
+def dense_on_device(tiles, tile_rows, tile_cols, tile_counts, start_panel):
+    n_row, n_col, n_sub = (lax.axis_size(name) for name in ("row", "col", "sub"))
+    slots, side, _ = tiles.shape
+    half_width = start_panel.shape[1]
+    width = half_width * n_sub
+    half = side // n_sub
+    devices = n_row * n_col * n_sub
+    nodes = n_row * n_col * side
+    in_vmem = pl.BlockSpec(memory_space=pltpu.VMEM)
+    in_smem = pl.BlockSpec(memory_space=pltpu.SMEM)
+    f32 = jnp.float32
+    dma = pltpu.SemaphoreType.DMA
+    return pl.pallas_call(
+        functools.partial(lanczos_kernel, n_row, n_col, n_sub),
+        out_shape=(
+            jax.ShapeDtypeStruct(start_panel.shape, f32),
+            jax.ShapeDtypeStruct((ITERS, width, width), f32),
+            jax.ShapeDtypeStruct((ITERS + 1, width, width), f32),
+        ),
+        in_specs=[in_smem, in_smem, in_smem, pl.BlockSpec(memory_space=pl.ANY), in_vmem],
+        out_specs=(in_vmem, in_vmem, in_vmem),
+        scratch_shapes=[
+            pltpu.VMEM((slots, half, side), f32),
+            pltpu.VMEM((n_col * half, slots // n_col * side), jnp.bfloat16),
+            pltpu.VMEM((n_col * half, slots // n_col * side), jnp.bfloat16),
+            pltpu.VMEM((devices, half_width, side), f32),
+            pltpu.VMEM((devices, 8, n_col * half), f32),
+            pltpu.VMEM((ITERS, devices, width, n_col * half), f32),
+            pltpu.VMEM((8, nodes), f32),
+            pltpu.VMEM((width, nodes), f32),
+            pltpu.VMEM((width, nodes), f32),
+            pltpu.VMEM((width, nodes), f32),
+            dma((slots,)),
+            dma((devices,)),
+            dma((devices,)),
+            dma((devices,)),
+            dma((devices,)),
+            dma((ITERS, devices)),
+            dma((ITERS, devices)),
+        ],
+        compiler_params=pltpu.CompilerParams(
+            collective_id=0, has_side_effects=True, vmem_limit_bytes=40 * 2**20
+        ),
+    )(tile_rows, tile_cols, tile_counts, tiles, start_panel)
+
+
+def on_one_device(tiles, tile_rows, tile_cols, tile_counts, start_panel):
+    tile_side = tiles.shape[1]
+    one_block = start_panel.shape[0] == tile_side
+    covered = tiles.shape[0] == lax.axis_size("row") * lax.axis_size("col")
+    form = dense_on_device if one_block and covered else on_device
+    return form(tiles, tile_rows, tile_cols, tile_counts, start_panel)
+
+
 def solution(mesh):
     return jax.shard_map(
-        on_device,
+        on_one_device,
         mesh=mesh,
         in_specs=(
             P(("parts", "row", "col"), None, None),

time: 404 us -> 72.2 us (0.18)
  the two profiles are of different devices: /device:TPU:0 before, /device:TPU:15 now
where the time goes in v1:
time: 72.2 us; the launch traced here: 72 us
  Pallas kernels  65 us (90%)
  local copies, waits for them, and re-layouts  5.64 us (8%)
  between operations  1.3 us (2%)
    pallas_call x1, Pallas kernels, dense_on_device(): pl.pallas_call(functools.partial(lanczos_kernel, n_row, n_col, n_sub), ou...  65 us
    unnamed x9, local copies, waits for them, and re-layouts  4.96 us

profile of v1, /device:TPU:15, one launch (start us, length us, event | category | flops | bytes accessed | tf_op | source)
XLA Modules:
  0.0 72.0 jit_solution(2830789550543122560)
XLA Ops:
  1.3 0.8 %copy.8.start_ref = f32[256,16]{1,0:T(8,128)S(1)} copy(f32[256,16]{0,1:T(8,128)} %param.9) | data formatting | bytes 32768 | tf_op args[4]
  2.1 0.0 copy-start
  2.1 1.6 %copy-done = f32[8,256,256]{2,1,0:T(8,128)S(1)} copy-done((f32[8,256,256]{2,1,0:T(8,128)S(1)}, f32[8,256,256]{2,1,0:T(8,128)}, u32[]{:S(2)}) %copy-start) | copy-done | bytes 2097176
  3.7 0.0 copy-start.1
  3.7 0.7 copy-done.1
  4.3 0.0 copy-start.2
  4.3 0.7 copy-done.2
  5.0 65.0 %shard_map.76 = (f32[256,16]{1,0:T(8,128)S(1)}, f32[3,32,32]{2,1,0:T(8,128)S(1)}, f32[4,32,32]{2,1,0:T(8,128)S(1)}) custom-call(s32[8]{0:T(128)S(1)} %copy-done.1, s32[8]{0:T(128)S(1)} %copy-done.2, s32[1]{0:T(128)S(6)} %copy.12.count_ref, f32[8,256,256]{2,1,0:T(8,128)S(1)} %copy-done, f32[256,16]{1,0:T(8,128)S(1)} %copy.8.start_ref), custom_call_target="tpu_custom_call" | custom-call | tf_op jit(solution)/shard_map/pallas_call | solution.py:332
  70.0 0.7 copy.9
  70.7 0.6 copy.13
  71.3 0.6 copy.14
Async XLA Ops:
  2.1 1.6 %copy-start = (f32[8,256,256]{2,1,0:T(8,128)S(1)}, f32[8,256,256]{2,1,0:T(8,128)}, u32[]{:S(2)}) copy-start(f32[8,256,256]{2,1,0:T(8,128)} %tiles_ref.1) | copy-start | bytes 6291460
  3.7 0.7 copy-start.1
  4.3 0.7 copy-start.2

commit v2 on v1

--- a/solution.py
+++ b/solution.py
@@ -149,30 +149,44 @@
     n_row, n_col, n_sub,
     rows_ref, cols_ref, count_ref, tiles_ref, start_ref,
     panel_ref, alphas_ref, betas_ref,
-    tiles_buf, tile_high, tile_low, start_buf, sums_buf, part_buf,
+    tiles_buf, tile_high, tile_low, start_buf, sums_buf, mine_buf, theirs_buf, piece_buf,
     root_ref, current_ref, previous_ref, residual_ref,
-    tile_sem, start_send, start_recv, sums_send, sums_recv, part_send, part_recv,
+    tile_sem, sums_send, sums_recv, start_send, start_recv, start_pass, start_took,
+    half_send, half_recv, piece_send, piece_recv, piece_pass, piece_took,
 ):
     slots, side, _ = tiles_ref.shape
     half = side // n_sub
     local_cols = slots // n_col
-    width = part_buf.shape[2]
+    width = current_ref.shape[1]
     half_width = width // n_sub
-    devices = n_row * n_col * n_sub
+    chips = n_row * n_col
+    devices = chips * n_sub
+    pieces = n_row * n_sub
+    span = n_col * half
     row = lax.axis_index("row")
     col = lax.axis_index("col")
     sub = lax.axis_index("sub")
-    me = (row * n_col + col) * n_sub + sub
-
-    def place(peer):
-        return {
-            "row": peer // (n_col * n_sub),
-            "col": (peer // n_sub) % n_col,
-            "sub": peer % n_sub,
-        }
-
-    def other(step):
-        return lax.rem(me + step, devices)
+    chip = row * n_col + col
+    me = chip * n_sub + sub
+
+    def chip_place(peer):
+        return {"row": peer // n_col, "col": lax.rem(peer, n_col), "sub": sub}
+
+    def remote(buf, index, send, recv, place):
+        return pltpu.make_async_remote_copy(
+            src_ref=buf.at[index],
+            dst_ref=buf.at[index],
+            send_sem=send,
+            recv_sem=recv,
+            device_id=place,
+            device_id_type=pl.DeviceIdType.MESH,
+        )
+
+    sent = []
+
+    def push(copy):
+        copy.start()
+        sent.append(copy)
 
     tile_copies = []
     for slot in range(slots):
@@ -184,49 +198,23 @@
         copy.start()
         tile_copies.append(copy)
 
+    def device_place(peer):
+        return {
+            "row": peer // (n_col * n_sub),
+            "col": lax.rem(peer // n_sub, n_col),
+            "sub": lax.rem(peer, n_sub),
+        }
+
     barrier = pltpu.get_barrier_semaphore()
     for step in range(1, devices):
         pl.semaphore_signal(
-            barrier, inc=1, device_id=place(other(step)), device_id_type=pl.DeviceIdType.MESH
+            barrier,
+            inc=1,
+            device_id=device_place(lax.rem(me + step, devices)),
+            device_id_type=pl.DeviceIdType.MESH,
         )
-    start_buf[me] = start_ref[...].T
-    pl.semaphore_wait(barrier, devices - 1)
-
-    def copies(buf, send, recv):
-        return [
-            pltpu.make_async_remote_copy(
-                src_ref=buf.at[me],
-                dst_ref=buf.at[me],
-                send_sem=send.at[step],
-                recv_sem=recv.at[me],
-                device_id=place(other(step)),
-                device_id_type=pl.DeviceIdType.MESH,
-            )
-            for step in range(1, devices)
-        ]
-
-    def send_all(buf, send, recv):
-        for copy in copies(buf, send, recv):
-            copy.start()
-
-    def wait_all(buf, send, recv):
-        for step in range(1, devices):
-            peer = other(step)
-            pltpu.make_async_remote_copy(
-                src_ref=buf.at[peer],
-                dst_ref=buf.at[peer],
-                send_sem=send.at[step],
-                recv_sem=recv.at[peer],
-                device_id=place(peer),
-                device_id_type=pl.DeviceIdType.MESH,
-            ).wait_recv()
-
-    def wait_sent(buf, send, recv):
-        for copy in copies(buf, send, recv):
-            copy.wait_send()
-
-    send_all(start_buf, start_send, start_recv)
-
+
+    start_buf[chip * n_sub + sub] = start_ref[...].T
     for copy in tile_copies:
         copy.wait()
     for block in range(n_col):
@@ -241,80 +229,178 @@
             tile_high[at] = high
             tile_low[at] = low
     ones = jnp.ones((8, local_cols * side), jnp.bfloat16)
-    sums_buf[me] = lax.dot_general(
+    sums = lax.dot_general(
         ones, tile_high[...], LAST, preferred_element_type=jnp.float32
     ) + lax.dot_general(ones, tile_low[...], LAST, preferred_element_type=jnp.float32)
-    send_all(sums_buf, sums_send, sums_recv)
-
-    wait_all(start_buf, start_send, start_recv)
-    for block in range(n_row * n_col):
-        for part in range(n_sub):
-            residual_ref[
-                part * half_width : (part + 1) * half_width, block * side : (block + 1) * side
-            ] = start_buf[block * n_sub + part]
-
-    def orthonormalize(at):
-        panel = residual_ref[...]
-        upper, inverse = triangular_parts(dot_last(panel, panel))
+    sums_buf[me] = sums[0:1]
+    pl.semaphore_wait(barrier, devices - 1)
+
+    for step in range(1, chips):
+        peer = lax.rem(chip + step, chips)
+        push(remote(start_buf, me, start_send.at[step], start_recv.at[chip], chip_place(peer)))
+    for step in range(1, n_sub):
+        peer = lax.rem(sub + step, n_sub)
+        push(remote(start_buf, me, start_pass.at[0, step], start_took.at[chip, sub], {"sub": peer}))
+    for step in range(1, devices):
+        peer = lax.rem(me + step, devices)
+        push(remote(sums_buf, me, sums_send.at[step], sums_recv.at[me], device_place(peer)))
+    for step in range(1, chips):
+        peer = lax.rem(chip + step, chips)
+        index = peer * n_sub + sub
+        remote(
+            start_buf, index, start_send.at[step], start_recv.at[peer], chip_place(peer)
+        ).wait_recv()
+        for hop in range(1, n_sub):
+            to = lax.rem(sub + hop, n_sub)
+            push(
+                remote(
+                    start_buf, index, start_pass.at[step, hop], start_took.at[peer, sub], {"sub": to}
+                )
+            )
+    for step in range(1, devices):
+        peer = lax.rem(me + step, devices)
+        remote(
+            sums_buf, peer, sums_send.at[step], sums_recv.at[peer], device_place(peer)
+        ).wait_recv()
+    for r in range(n_row):
+        for s in range(n_sub):
+            total = sums_buf[(r * n_col) * n_sub + s]
+            for c in range(1, n_col):
+                total = total + sums_buf[(r * n_col + c) * n_sub + s]
+            root_ref[r * n_sub + s] = 1.0 / jnp.sqrt(1.0 + total)
+    for hop in range(1, n_sub):
+        source = lax.rem(sub + hop, n_sub)
+        for step in range(chips):
+            peer = lax.rem(chip + step, chips)
+            remote(
+                start_buf, peer * n_sub + source, start_pass.at[step, hop],
+                start_took.at[peer, source], {"sub": source},
+            ).wait_recv()
+    for r in range(n_row):
+        for c in range(n_col):
+            for part in range(n_sub):
+                for s in range(n_sub):
+                    residual_ref[
+                        r * n_sub + s,
+                        part * half_width : (part + 1) * half_width,
+                        c * half : (c + 1) * half,
+                    ] = start_buf[(r * n_col + c) * n_sub + part, :, s * half : (s + 1) * half]
+
+    def factorize_residual(at):
+        gram = jnp.zeros((width, width), jnp.float32)
+        for p in range(pieces):
+            gram = gram + dot_last(residual_ref[p], residual_ref[p])
+        upper, inverse = triangular_parts(gram)
         betas_ref[at] = upper
-        current_ref[...] = full_dot(inverse, panel)
-        return upper
-
-    beta = orthonormalize(0)
-
-    def assemble(buf, target, finish):
-        for r in range(n_row):
-            for s in range(n_sub):
-                total = buf[(r * n_col) * n_sub + s]
-                for c in range(1, n_col):
-                    total = total + buf[(r * n_col + c) * n_sub + s]
-                for block in range(n_col):
-                    first = (r * n_col + block) * side + s * half
-                    target[:, first : first + half] = finish(
-                        total[:, block * half : (block + 1) * half], first
-                    )
-
-    wait_all(sums_buf, sums_send, sums_recv)
-    assemble(sums_buf, root_ref, lambda total, first: 1.0 / jnp.sqrt(1.0 + total))
-
+        return upper, inverse
+
+    def orthonormalize(inverse):
+        for p in range(pieces):
+            current_ref[p] = full_dot(inverse, residual_ref[p])
+
+    own_lanes = pl.ds(pl.multiple_of(col * half, half), half)
+    own_piece = row * n_sub + sub
+    root_own = root_ref[own_piece]
     for iteration in range(alphas_ref.shape[0]):
         highs, lows = [], []
-        for column in range(local_cols):
-            at = pl.ds(pl.multiple_of((column * n_col + col) * side, side), side)
-            high, low = split_two(current_ref[:, at] * root_ref[0:1, at])
+        for p in range(pieces):
+            high, low = split_two(residual_ref[p, :, own_lanes] * root_ref[p, :, own_lanes])
             highs.append(high)
             lows.append(low)
         high = jnp.concatenate(highs, axis=1)
         both = jnp.concatenate([high, jnp.concatenate(lows, axis=1)], axis=0)
         first = lax.dot_general(both, tile_high[...], LAST, preferred_element_type=jnp.float32)
         second = lax.dot_general(high, tile_low[...], LAST, preferred_element_type=jnp.float32)
-        buf = part_buf.at[iteration]
-        send = part_send.at[iteration]
-        recv = part_recv.at[iteration]
-        buf[me] = first[:width] + (first[width:] + second)
-        send_all(buf, send, recv)
-        wait_all(buf, send, recv)
-        assemble(
-            buf, residual_ref, lambda total, first: total * root_ref[0:1, first : first + half]
-        )
-        residual = residual_ref[...]
+        halves = theirs_buf.at[iteration]
+        halves[col] = first[:width] + (first[width:] + second)
+        for step in range(1, n_col):
+            peer = lax.rem(col + step, n_col)
+            push(
+                remote(
+                    halves, col, half_send.at[iteration, step], half_recv.at[iteration, col],
+                    {"col": peer},
+                )
+            )
+        upper, inverse = factorize_residual(iteration)
+        for step in range(1, n_col):
+            peer = lax.rem(col + step, n_col)
+            remote(
+                halves, peer, half_send.at[iteration, step], half_recv.at[iteration, peer],
+                {"col": peer},
+            ).wait_recv()
+        total = halves[0]
+        for c in range(1, n_col):
+            total = total + halves[c]
+        got = piece_buf.at[iteration]
+        got[own_piece] = total * root_own
+        for step in range(1, n_row):
+            peer = lax.rem(row + step, n_row)
+            push(
+                remote(
+                    got, own_piece, piece_send.at[iteration, step],
+                    piece_recv.at[iteration, row], {"row": peer},
+                )
+            )
+        for hop in range(1, n_sub):
+            to = lax.rem(sub + hop, n_sub)
+            push(
+                remote(
+                    got, own_piece, piece_pass.at[iteration, 0, hop],
+                    piece_took.at[iteration, row, sub], {"sub": to},
+                )
+            )
         if iteration > 0:
-            residual = residual - full_dot(beta, previous_ref[...])
-        current = current_ref[...]
-        alpha = dot_last(current, residual)
+            for p in range(pieces):
+                previous_ref[p] = current_ref[p]
+        orthonormalize(inverse)
+        for step in range(1, n_row):
+            peer = lax.rem(row + step, n_row)
+            index = peer * n_sub + sub
+            remote(
+                got, index, piece_send.at[iteration, step], piece_recv.at[iteration, peer],
+                {"row": peer},
+            ).wait_recv()
+            for hop in range(1, n_sub):
+                to = lax.rem(sub + hop, n_sub)
+                push(
+                    remote(
+                        got, index, piece_pass.at[iteration, step, hop],
+                        piece_took.at[iteration, peer, sub], {"sub": to},
+                    )
+                )
+        for hop in range(1, n_sub):
+            source = lax.rem(sub + hop, n_sub)
+            for step in range(n_row):
+                peer = lax.rem(row + step, n_row)
+                remote(
+                    got, peer * n_sub + source, piece_pass.at[iteration, step, hop],
+                    piece_took.at[iteration, peer, source], {"sub": source},
+                ).wait_recv()
+        alpha = jnp.zeros((width, width), jnp.float32)
+        for p in range(pieces):
+            if iteration > 0:
+                mixed = full_dot(
+                    jnp.concatenate([inverse, -upper], axis=1),
+                    jnp.concatenate([got[p], previous_ref[p]], axis=0),
+                )
+            else:
+                mixed = full_dot(inverse, got[p])
+            residual_ref[p] = mixed
+            alpha = alpha + dot_last(current_ref[p], mixed)
         alphas_ref[iteration] = alpha
-        residual_ref[...] = residual - full_dot(alpha.T, current)
-        previous_ref[...] = current
-        beta = orthonormalize(iteration + 1)
-
-    own = pl.ds(pl.multiple_of((row * n_col + col) * side, side), side)
+        turned = alpha.T
+        for p in range(pieces):
+            residual_ref[p] = residual_ref[p] - full_dot(turned, current_ref[p])
+
+    _, inverse = factorize_residual(alphas_ref.shape[0])
     rows_own = pl.ds(pl.multiple_of(sub * half_width, half_width), half_width)
-    panel_ref[...] = current_ref[rows_own, own].T
-
-    wait_sent(start_buf, start_send, start_recv)
-    wait_sent(sums_buf, sums_send, sums_recv)
-    for iteration in range(alphas_ref.shape[0]):
-        wait_sent(part_buf.at[iteration], part_send.at[iteration], part_recv.at[iteration])
+    mine_buf[...] = inverse
+    for s in range(n_sub):
+        panel_ref[s * half : (s + 1) * half, :] = full_dot(
+            mine_buf[rows_own, :], residual_ref[row * n_sub + s, :, own_lanes]
+        ).T
+    for copy in sent:
+        copy.wait_send()
 
 
 def dense_on_device(tiles, tile_rows, tile_cols, tile_counts, start_panel):
@@ -324,7 +410,9 @@
     width = half_width * n_sub
     half = side // n_sub
     devices = n_row * n_col * n_sub
-    nodes = n_row * n_col * side
+    chips = n_row * n_col
+    pieces = n_row * n_sub
+    span = n_col * half
     in_vmem = pl.BlockSpec(memory_space=pltpu.VMEM)
     in_smem = pl.BlockSpec(memory_space=pltpu.SMEM)
     f32 = jnp.float32
@@ -340,22 +428,30 @@
         out_specs=(in_vmem, in_vmem, in_vmem),
         scratch_shapes=[
             pltpu.VMEM((slots, half, side), f32),
-            pltpu.VMEM((n_col * half, slots // n_col * side), jnp.bfloat16),
-            pltpu.VMEM((n_col * half, slots // n_col * side), jnp.bfloat16),
+            pltpu.VMEM((span, slots // n_col * side), jnp.bfloat16),
+            pltpu.VMEM((span, slots // n_col * side), jnp.bfloat16),
             pltpu.VMEM((devices, half_width, side), f32),
-            pltpu.VMEM((devices, 8, n_col * half), f32),
-            pltpu.VMEM((ITERS, devices, width, n_col * half), f32),
-            pltpu.VMEM((8, nodes), f32),
-            pltpu.VMEM((width, nodes), f32),
-            pltpu.VMEM((width, nodes), f32),
-            pltpu.VMEM((width, nodes), f32),
+            pltpu.VMEM((devices, 1, span), f32),
+            pltpu.VMEM((width, width), f32),
+            pltpu.VMEM((ITERS, n_col, width, span), f32),
+            pltpu.VMEM((ITERS, pieces, width, span), f32),
+            pltpu.VMEM((pieces, 1, span), f32),
+            pltpu.VMEM((pieces, width, span), f32),
+            pltpu.VMEM((pieces, width, span), f32),
+            pltpu.VMEM((pieces, width, span), f32),
             dma((slots,)),
             dma((devices,)),
             dma((devices,)),
-            dma((devices,)),
-            dma((devices,)),
-            dma((ITERS, devices)),
-            dma((ITERS, devices)),
+            dma((chips,)),
+            dma((chips,)),
+            dma((chips, n_sub)),
+            dma((chips, n_sub)),
+            dma((ITERS, n_col)),
+            dma((ITERS, n_col)),
+            dma((ITERS, n_row)),
+            dma((ITERS, n_row)),
+            dma((ITERS, n_row, n_sub)),
+            dma((ITERS, n_row, n_sub)),
         ],
         compiler_params=pltpu.CompilerParams(
             collective_id=0, has_side_effects=True, vmem_limit_bytes=40 * 2**20

time: 72.2 us -> 53.6 us (0.74)
  the two profiles are of different devices: /device:TPU:15 before, /device:TPU:1 now
where the time goes in v2:
time: 53.6 us; the launch traced here: 53.4 us
  Pallas kernels  46.4 us (87%)
  local copies, waits for them, and re-layouts  5.64 us (11%)
  between operations  1.3 us (2%)
    pallas_call x1, Pallas kernels, dense_on_device(): pl.pallas_call(functools.partial(lanczos_kernel, n_row, n_col, n_sub), ou...  46.4 us
    unnamed x9, local copies, waits for them, and re-layouts  4.96 us

profile of v2, /device:TPU:1, one launch (start us, length us, event | category | flops | bytes accessed | tf_op | source)
XLA Modules:
  0.0 53.4 jit_solution(10647864349692434705)
XLA Ops:
  1.3 0.8 %copy.8.start_ref = f32[256,16]{1,0:T(8,128)S(1)} copy(f32[256,16]{0,1:T(8,128)} %param.9) | data formatting | bytes 32768 | tf_op args[4]
  2.1 0.0 copy-start
  2.1 1.6 %copy-done = f32[8,256,256]{2,1,0:T(8,128)S(1)} copy-done((f32[8,256,256]{2,1,0:T(8,128)S(1)}, f32[8,256,256]{2,1,0:T(8,128)}, u32[]{:S(2)}) %copy-start) | copy-done | bytes 2097176
  3.7 0.0 copy-start.1
  3.7 0.7 %copy-done.1 = s32[8]{0:T(128)S(1)} copy-done((s32[8]{0:T(128)S(1)}, s32[8]{0:T(128)}, u32[]{:S(2)}) %copy-start.1) | copy-done | bytes 56
  4.3 0.0 copy-start.2
  4.3 0.7 %copy-done.2 = s32[8]{0:T(128)S(1)} copy-done((s32[8]{0:T(128)S(1)}, s32[8]{0:T(128)}, u32[]{:S(2)}) %copy-start.2) | copy-done | bytes 56
  5.0 46.4 %shard_map.76 = (f32[256,16]{1,0:T(8,128)S(1)}, f32[3,32,32]{2,1,0:T(8,128)S(1)}, f32[4,32,32]{2,1,0:T(8,128)S(1)}) custom-call(s32[8]{0:T(128)S(1)} %copy-done.1, s32[8]{0:T(128)S(1)} %copy-done.2, s32[1]{0:T(128)S(6)} %copy.12.count_ref, f32[8,256,256]{2,1,0:T(8,128)S(1)} %copy-done, f32[256,16]{1,0:T(8,128)S(1)} %copy.8.start_ref), custom_call_target="tpu_custom_call" | custom-call | tf_op jit(solution)/shard_map/pallas_call | solution.py:420
  51.5 0.7 %copy.9 = f32[256,16]{0,1:T(8,128)} copy(f32[256,16]{1,0:T(8,128)S(1)} %get-tuple-element.3) | data formatting | bytes 32768 | tf_op jit(solution)/shard_map/pallas_call | solution.py:420
  52.1 0.6 %copy.13 = f32[3,32,32]{2,1,0:T(8,128)} copy(f32[3,32,32]{2,1,0:T(8,128)S(1)} %get-tuple-element.10) | data formatting | bytes 24576
  52.8 0.6 %copy.14 = f32[4,32,32]{2,1,0:T(8,128)} copy(f32[4,32,32]{2,1,0:T(8,128)S(1)} %get-tuple-element.11) | data formatting | bytes 32768
Async XLA Ops:
  2.1 1.6 %copy-start = (f32[8,256,256]{2,1,0:T(8,128)S(1)}, f32[8,256,256]{2,1,0:T(8,128)}, u32[]{:S(2)}) copy-start(f32[8,256,256]{2,1,0:T(8,128)} %tiles_ref.1) | copy-start | bytes 6291460
  3.7 0.7 %copy-start.1 = (s32[8]{0:T(128)S(1)}, s32[8]{0:T(128)}, u32[]{:S(2)}) copy-start(s32[8]{0:T(128)} %rows_ref.1) | copy-start | bytes 100
  4.3 0.7 %copy-start.2 = (s32[8]{0:T(128)S(1)}, s32[8]{0:T(128)}, u32[]{:S(2)}) copy-start(s32[8]{0:T(128)} %cols_ref.1) | copy-start | bytes 100

commit v3 on v2

--- a/solution.py
+++ b/solution.py
@@ -147,11 +147,12 @@
 
 def lanczos_kernel(
     n_row, n_col, n_sub,
-    rows_ref, cols_ref, count_ref, tiles_ref, start_ref,
+    rows_any, cols_any, count_any, tiles_ref, start_ref,
     panel_ref, alphas_ref, betas_ref,
-    tiles_buf, tile_high, tile_low, start_buf, sums_buf, mine_buf, theirs_buf, piece_buf,
+    rows_ref, cols_ref, count_ref, small_sem, tiles_buf, tile_high, tile_low, start_buf, sums_buf, mine_buf, theirs_buf, piece_buf,
     root_ref, current_ref, previous_ref, residual_ref,
-    tile_sem, sums_send, sums_recv, start_send, start_recv, start_pass, start_took,
+    tile_sem, sums_send, sums_recv, root_send, root_recv, root_pass, root_took,
+    start_x_send, start_x_recv, start_send, start_recv, start_pass, start_took,
     half_send, half_recv, piece_send, piece_recv, piece_pass, piece_took,
 ):
     slots, side, _ = tiles_ref.shape
@@ -160,17 +161,12 @@
     width = current_ref.shape[1]
     half_width = width // n_sub
     chips = n_row * n_col
-    devices = chips * n_sub
     pieces = n_row * n_sub
     span = n_col * half
     row = lax.axis_index("row")
     col = lax.axis_index("col")
     sub = lax.axis_index("sub")
     chip = row * n_col + col
-    me = chip * n_sub + sub
-
-    def chip_place(peer):
-        return {"row": peer // n_col, "col": lax.rem(peer, n_col), "sub": sub}
 
     def remote(buf, index, send, recv, place):
         return pltpu.make_async_remote_copy(
@@ -188,6 +184,19 @@
         copy.start()
         sent.append(copy)
 
+    small_copies = [
+        pltpu.make_async_copy(source, target, small_sem.at[at])
+        for at, (source, target) in enumerate(
+            (
+                (rows_any, rows_ref),
+                (cols_any, cols_ref),
+                (count_any, count_ref),
+                (start_ref, start_buf.at[chip, sub]),
+            )
+        )
+    ]
+    for copy in small_copies:
+        copy.start()
     tile_copies = []
     for slot in range(slots):
         copy = pltpu.make_async_copy(
@@ -198,24 +207,21 @@
         copy.start()
         tile_copies.append(copy)
 
-    def device_place(peer):
-        return {
-            "row": peer // (n_col * n_sub),
-            "col": lax.rem(peer // n_sub, n_col),
-            "sub": lax.rem(peer, n_sub),
-        }
-
+    rows_apart = [lax.rem(row + step, n_row) for step in range(1, n_row)]
+    cols_apart = [lax.rem(col + step, n_col) for step in range(1, n_col)]
+    subs_apart = [lax.rem(sub + step, n_sub) for step in range(1, n_sub)]
+    partners = (
+        [{"row": peer} for peer in rows_apart]
+        + [{"col": peer} for peer in cols_apart]
+        + [{"sub": peer} for peer in subs_apart]
+    )
     barrier = pltpu.get_barrier_semaphore()
-    for step in range(1, devices):
+    for partner in partners:
         pl.semaphore_signal(
-            barrier,
-            inc=1,
-            device_id=device_place(lax.rem(me + step, devices)),
-            device_id_type=pl.DeviceIdType.MESH,
-        )
-
-    start_buf[chip * n_sub + sub] = start_ref[...].T
-    for copy in tile_copies:
+            barrier, inc=1, device_id=partner, device_id_type=pl.DeviceIdType.MESH
+        )
+
+    for copy in small_copies + tile_copies:
         copy.wait()
     for block in range(n_col):
         for column in range(local_cols):
@@ -232,50 +238,113 @@
     sums = lax.dot_general(
         ones, tile_high[...], LAST, preferred_element_type=jnp.float32
     ) + lax.dot_general(ones, tile_low[...], LAST, preferred_element_type=jnp.float32)
-    sums_buf[me] = sums[0:1]
-    pl.semaphore_wait(barrier, devices - 1)
-
-    for step in range(1, chips):
-        peer = lax.rem(chip + step, chips)
-        push(remote(start_buf, me, start_send.at[step], start_recv.at[chip], chip_place(peer)))
-    for step in range(1, n_sub):
-        peer = lax.rem(sub + step, n_sub)
-        push(remote(start_buf, me, start_pass.at[0, step], start_took.at[chip, sub], {"sub": peer}))
-    for step in range(1, devices):
-        peer = lax.rem(me + step, devices)
-        push(remote(sums_buf, me, sums_send.at[step], sums_recv.at[me], device_place(peer)))
-    for step in range(1, chips):
-        peer = lax.rem(chip + step, chips)
-        index = peer * n_sub + sub
-        remote(
-            start_buf, index, start_send.at[step], start_recv.at[peer], chip_place(peer)
+    sums_buf[col] = sums[0:1]
+    pl.semaphore_wait(barrier, len(partners))
+
+    def start_from(source_row, source_col, source_sub):
+        return start_buf.at[source_row * n_col + source_col, source_sub]
+
+    def move(ref, send, recv, place):
+        return pltpu.make_async_remote_copy(
+            src_ref=ref,
+            dst_ref=ref,
+            send_sem=send,
+            recv_sem=recv,
+            device_id=place,
+            device_id_type=pl.DeviceIdType.MESH,
+        )
+
+    def start_along_cols(step, source_col):
+        return move(
+            start_from(row, source_col, sub), start_x_send.at[step], start_x_recv.at[source_col],
+            {"col": cols_apart[step]},
+        )
+
+    def start_along_rows(step, source_row, source_col):
+        return move(
+            start_from(source_row, source_col, sub),
+            start_send.at[step, source_col],
+            start_recv.at[source_row, source_col],
+            {"row": rows_apart[step]},
+        )
+
+    def start_along_subs(step, source_row, source_col, source_sub):
+        return move(
+            start_from(source_row, source_col, source_sub),
+            start_pass.at[step, source_row, source_col],
+            start_took.at[source_row, source_col, source_sub],
+            {"sub": subs_apart[step]},
+        )
+
+    for step in range(n_col - 1):
+        push(
+            move(
+                sums_buf.at[col], sums_send.at[step], sums_recv.at[col], {"col": cols_apart[step]}
+            )
+        )
+        push(start_along_cols(step, col))
+    for step in range(n_row - 1):
+        push(start_along_rows(step, row, col))
+    for step in range(n_sub - 1):
+        push(start_along_subs(step, row, col, sub))
+
+    for step in range(n_col - 1):
+        peer = cols_apart[step]
+        move(
+            sums_buf.at[peer], sums_send.at[step], sums_recv.at[peer], {"col": peer}
         ).wait_recv()
-        for hop in range(1, n_sub):
-            to = lax.rem(sub + hop, n_sub)
-            push(
-                remote(
-                    start_buf, index, start_pass.at[step, hop], start_took.at[peer, sub], {"sub": to}
-                )
-            )
-    for step in range(1, devices):
-        peer = lax.rem(me + step, devices)
-        remote(
-            sums_buf, peer, sums_send.at[step], sums_recv.at[peer], device_place(peer)
-        ).wait_recv()
-    for r in range(n_row):
-        for s in range(n_sub):
-            total = sums_buf[(r * n_col) * n_sub + s]
-            for c in range(1, n_col):
-                total = total + sums_buf[(r * n_col + c) * n_sub + s]
-            root_ref[r * n_sub + s] = 1.0 / jnp.sqrt(1.0 + total)
-    for hop in range(1, n_sub):
-        source = lax.rem(sub + hop, n_sub)
-        for step in range(chips):
-            peer = lax.rem(chip + step, chips)
-            remote(
-                start_buf, peer * n_sub + source, start_pass.at[step, hop],
-                start_took.at[peer, source], {"sub": source},
-            ).wait_recv()
+    total = sums_buf[0]
+    for c in range(1, n_col):
+        total = total + sums_buf[c]
+    root_own = 1.0 / jnp.sqrt(1.0 + total)
+    own_piece = row * n_sub + sub
+
+    def root_along_rows(step, source_row):
+        return move(
+            root_ref.at[source_row * n_sub + sub], root_send.at[step], root_recv.at[source_row],
+            {"row": rows_apart[step]},
+        )
+
+    def root_along_subs(step, source_row, source_sub):
+        return move(
+            root_ref.at[source_row * n_sub + source_sub],
+            root_pass.at[step, source_row],
+            root_took.at[source_row, source_sub],
+            {"sub": subs_apart[step]},
+        )
+
+    root_ref[own_piece] = root_own
+    for step in range(n_row - 1):
+        push(root_along_rows(step, row))
+    for step in range(n_sub - 1):
+        push(root_along_subs(step, row, sub))
+    for step in range(n_col - 1):
+        peer = cols_apart[step]
+        start_along_cols(step, peer).wait_recv()
+        for hop in range(n_row - 1):
+            push(start_along_rows(hop, row, peer))
+        for hop in range(n_sub - 1):
+            push(start_along_subs(hop, row, peer, sub))
+    for step in range(n_row - 1):
+        peer = rows_apart[step]
+        root_along_rows(step, peer).wait_recv()
+        for hop in range(n_sub - 1):
+            push(root_along_subs(hop, peer, sub))
+        start_along_rows(step, peer, col).wait_recv()
+        for hop in range(n_sub - 1):
+            push(start_along_subs(hop, peer, col, sub))
+    for step in range(n_row - 1):
+        peer = rows_apart[step]
+        for source_col in cols_apart:
+            start_along_rows(step, peer, source_col).wait_recv()
+            for hop in range(n_sub - 1):
+                push(start_along_subs(hop, peer, source_col, sub))
+    for step in range(n_sub - 1):
+        source = subs_apart[step]
+        for peer in [row] + rows_apart:
+            root_along_subs(step, peer, source).wait_recv()
+            for source_col in [col] + cols_apart:
+                start_along_subs(step, peer, source_col, source).wait_recv()
     for r in range(n_row):
         for c in range(n_col):
             for part in range(n_sub):
@@ -284,7 +353,7 @@
                         r * n_sub + s,
                         part * half_width : (part + 1) * half_width,
                         c * half : (c + 1) * half,
-                    ] = start_buf[(r * n_col + c) * n_sub + part, :, s * half : (s + 1) * half]
+                    ] = start_buf[r * n_col + c, part, :, s * half : (s + 1) * half]
 
     def factorize_residual(at):
         gram = jnp.zeros((width, width), jnp.float32)
@@ -299,8 +368,6 @@
             current_ref[p] = full_dot(inverse, residual_ref[p])
 
     own_lanes = pl.ds(pl.multiple_of(col * half, half), half)
-    own_piece = row * n_sub + sub
-    root_own = root_ref[own_piece]
     for iteration in range(alphas_ref.shape[0]):
         highs, lows = [], []
         for p in range(pieces):
@@ -396,11 +463,45 @@
     rows_own = pl.ds(pl.multiple_of(sub * half_width, half_width), half_width)
     mine_buf[...] = inverse
     for s in range(n_sub):
-        panel_ref[s * half : (s + 1) * half, :] = full_dot(
+        panel_ref[:, s * half : (s + 1) * half] = full_dot(
             mine_buf[rows_own, :], residual_ref[row * n_sub + s, :, own_lanes]
-        ).T
+        )
     for copy in sent:
         copy.wait_send()
+
+
+def hand_out_kernel(*refs):
+    count = len(refs) // 3
+    sources, targets, held = refs[:count], refs[count : 2 * count], refs[2 * count : 3 * count]
+    sem = refs[-1]
+    inward = [
+        pltpu.make_async_copy(source, here, sem.at[0, at])
+        for at, (source, here) in enumerate(zip(sources, held))
+    ]
+    outward = [
+        pltpu.make_async_copy(here, target, sem.at[1, at])
+        for at, (here, target) in enumerate(zip(held, targets))
+    ]
+    for copy in inward:
+        copy.start()
+    for copy, onward in zip(inward, outward):
+        copy.wait()
+        onward.start()
+    for copy in outward:
+        copy.wait()
+
+
+def hand_out(*arrays):
+    in_hbm = pl.BlockSpec(memory_space=pltpu.HBM)
+    return pl.pallas_call(
+        hand_out_kernel,
+        out_shape=tuple(jax.ShapeDtypeStruct(array.shape, array.dtype) for array in arrays),
+        in_specs=[in_hbm] * len(arrays),
+        out_specs=(in_hbm,) * len(arrays),
+        scratch_shapes=[pltpu.VMEM(array.shape, array.dtype) for array in arrays]
+        + [pltpu.SemaphoreType.DMA((2, len(arrays)))],
+        compiler_params=pltpu.CompilerParams(vmem_limit_bytes=60 * 2**20),
+    )(*arrays)
 
 
 def dense_on_device(tiles, tile_rows, tile_cols, tile_counts, start_panel):
@@ -409,29 +510,31 @@
     half_width = start_panel.shape[1]
     width = half_width * n_sub
     half = side // n_sub
-    devices = n_row * n_col * n_sub
     chips = n_row * n_col
     pieces = n_row * n_sub
     span = n_col * half
     in_vmem = pl.BlockSpec(memory_space=pltpu.VMEM)
-    in_smem = pl.BlockSpec(memory_space=pltpu.SMEM)
     f32 = jnp.float32
     dma = pltpu.SemaphoreType.DMA
-    return pl.pallas_call(
+    panel, alphas, betas = pl.pallas_call(
         functools.partial(lanczos_kernel, n_row, n_col, n_sub),
         out_shape=(
-            jax.ShapeDtypeStruct(start_panel.shape, f32),
+            jax.ShapeDtypeStruct((half_width, side), f32),
             jax.ShapeDtypeStruct((ITERS, width, width), f32),
             jax.ShapeDtypeStruct((ITERS + 1, width, width), f32),
         ),
-        in_specs=[in_smem, in_smem, in_smem, pl.BlockSpec(memory_space=pl.ANY), in_vmem],
+        in_specs=[pl.BlockSpec(memory_space=pltpu.HBM)] * 5,
         out_specs=(in_vmem, in_vmem, in_vmem),
         scratch_shapes=[
+            pltpu.SMEM(tile_rows.shape, jnp.int32),
+            pltpu.SMEM(tile_cols.shape, jnp.int32),
+            pltpu.SMEM(tile_counts.shape, jnp.int32),
+            dma((4,)),
             pltpu.VMEM((slots, half, side), f32),
             pltpu.VMEM((span, slots // n_col * side), jnp.bfloat16),
             pltpu.VMEM((span, slots // n_col * side), jnp.bfloat16),
-            pltpu.VMEM((devices, half_width, side), f32),
-            pltpu.VMEM((devices, 1, span), f32),
+            pltpu.VMEM((chips, n_sub, half_width, side), f32),
+            pltpu.VMEM((n_col, 1, span), f32),
             pltpu.VMEM((width, width), f32),
             pltpu.VMEM((ITERS, n_col, width, span), f32),
             pltpu.VMEM((ITERS, pieces, width, span), f32),
@@ -440,12 +543,18 @@
             pltpu.VMEM((pieces, width, span), f32),
             pltpu.VMEM((pieces, width, span), f32),
             dma((slots,)),
-            dma((devices,)),
-            dma((devices,)),
-            dma((chips,)),
-            dma((chips,)),
-            dma((chips, n_sub)),
-            dma((chips, n_sub)),
+            dma((n_col,)),
+            dma((n_col,)),
+            dma((n_row,)),
+            dma((n_row,)),
+            dma((n_sub, n_row)),
+            dma((n_row, n_sub)),
+            dma((n_col,)),
+            dma((n_col,)),
+            dma((n_row, n_col)),
+            dma((n_row, n_col)),
+            dma((n_sub, n_row, n_col)),
+            dma((n_row, n_col, n_sub)),
             dma((ITERS, n_col)),
             dma((ITERS, n_col)),
             dma((ITERS, n_row)),
@@ -454,9 +563,11 @@
             dma((ITERS, n_row, n_sub)),
         ],
         compiler_params=pltpu.CompilerParams(
-            collective_id=0, has_side_effects=True, vmem_limit_bytes=40 * 2**20
+            collective_id=0, has_side_effects=True, vmem_limit_bytes=60 * 2**20
         ),
-    )(tile_rows, tile_cols, tile_counts, tiles, start_panel)
+    )(tile_rows, tile_cols, tile_counts, tiles, start_panel.T)
+    panel, alphas, betas = hand_out(panel, alphas, betas)
+    return panel.T, alphas, betas
 
 
 def on_one_device(tiles, tile_rows, tile_cols, tile_counts, start_panel):

time: 53.6 us -> 48.4 us (0.903)
  local copies, waits for them, and re-layouts: 5.64 us -> 0 us
    unnamed x9 -> x0, local copies, waits for them, and re-layouts: 4.96 us -> none
    pallas_call x0 -> x1, Pallas kernels: none -> 1.57 us  [hand_out(): pl.pallas_call(hand_out_kernel, out_shape=tuple((jax.ShapeDtypeStruct(arr...]
    pallas_call x1, Pallas kernels: 46.4 us -> 45.3 us  [dense_on_device(): pl.pallas_call(functools.partial(lanczos_kernel, n_row, n_col, n_sub), ou...]
    pallas_call x1 -> x0, local copies, waits for them, and re-layouts: 0.68 us -> none  [dense_on_device(): pl.pallas_call(functools.partial(lanczos_kernel, n_row, n_col, n_sub), ou...]
where the time goes in v3:
time: 48.4 us; the launch traced here: 48.1 us
  Pallas kernels  46.9 us (97%)
  between operations  1.29 us (3%)
    pallas_call x1, Pallas kernels, dense_on_device(): pl.pallas_call(functools.partial(lanczos_kernel, n_row, n_col, n_sub), ou...  45.3 us
    pallas_call x1, Pallas kernels, hand_out(): pl.pallas_call(hand_out_kernel, out_shape=tuple((jax.ShapeDtypeStruct(arr...  1.57 us

profile of v3, /device:TPU:1, one launch (start us, length us, event | category | flops | bytes accessed | tf_op | source)
XLA Modules:
  0.0 48.1 jit_solution(10744033890734369038)
XLA Ops:
  1.3 45.3 %shard_map.76 = (f32[16,256]{1,0:T(8,128)}, f32[3,32,32]{2,1,0:T(8,128)}, f32[4,32,32]{2,1,0:T(8,128)}) custom-call(s32[8]{0:T(128)} %rows_any.1, s32[8]{0:T(128)} %cols_any.1, s32[1]{0:T(128)S(6)} %copy.8.count_any, f32[8,256,256]{2,1,0:T(8,128)} %tiles_ref.1, f32[16,256]{1,0:T(8,128)} %bitcast.2), custom_call_target="tpu_custom_call" | custom-call | tf_op jit(solution)/shard_map/pallas_call | solution.py:519
  46.6 1.6 %shard_map.77 = (f32[16,256]{1,0:T(8,128)}, f32[3,32,32]{2,1,0:T(8,128)}, f32[4,32,32]{2,1,0:T(8,128)}) custom-call(f32[16,256]{1,0:T(8,128)} %get-tuple-element.9.refs_0_, f32[3,32,32]{2,1,0:T(8,128)} %get-tuple-element.10.refs_1_, f32[4,32,32]{2,1,0:T(8,128)} %get-tuple-element.11.refs_2_), custom_call_target="tpu_custom_call" | custom-call | tf_op jit(solution)/shard_map/pallas_call | solution.py:496

commit v4 on v2

--- a/solution.py
+++ b/solution.py
@@ -104,12 +104,22 @@
 
 
 LAST = (((1,), (1,)), ((), ()))
+PLAIN = (((1,), (0,)), ((), ()))
+
+
+def dot_parts(left, right, dims):
+    left_high, left_low = split_two(left)
+    right_high, right_low = split_two(right)
+    dot = functools.partial(
+        lax.dot_general, dimension_numbers=dims, preferred_element_type=jnp.float32
+    )
+    both = dot(jnp.concatenate([left_high, left_low], axis=0), right_high)
+    rows = left.shape[0]
+    return both[:rows] + (both[rows:] + dot(left_high, right_low))
 
 
 def dot_last(left, right):
-    return lax.dot_general(
-        left, right, LAST, precision=lax.Precision.HIGHEST, preferred_element_type=jnp.float32
-    )
+    return dot_parts(left, right, LAST)
 
 
 def split_two(value):
@@ -145,11 +155,15 @@
     return jnp.where(lanes >= rows, upper * scale, 0.0), inverse * scale
 
 
+def plain_dot(left, right):
+    return dot_parts(left, right, PLAIN)
+
+
 def lanczos_kernel(
     n_row, n_col, n_sub,
-    rows_ref, cols_ref, count_ref, tiles_ref, start_ref,
+    rows_any, cols_any, count_any, tiles_ref, start_ref,
     panel_ref, alphas_ref, betas_ref,
-    tiles_buf, tile_high, tile_low, start_buf, sums_buf, mine_buf, theirs_buf, piece_buf,
+    rows_ref, cols_ref, count_ref, small_sem, tiles_buf, tile_high, tile_low, start_buf, sums_buf, mine_buf, theirs_buf, piece_buf,
     root_ref, current_ref, previous_ref, residual_ref,
     tile_sem, sums_send, sums_recv, start_send, start_recv, start_pass, start_took,
     half_send, half_recv, piece_send, piece_recv, piece_pass, piece_took,
@@ -188,6 +202,19 @@
         copy.start()
         sent.append(copy)
 
+    small_copies = [
+        pltpu.make_async_copy(source, target, small_sem.at[at])
+        for at, (source, target) in enumerate(
+            (
+                (rows_any, rows_ref),
+                (cols_any, cols_ref),
+                (count_any, count_ref),
+                (start_ref, start_buf.at[me]),
+            )
+        )
+    ]
+    for copy in small_copies:
+        copy.start()
     tile_copies = []
     for slot in range(slots):
         copy = pltpu.make_async_copy(
@@ -214,8 +241,7 @@
             device_id_type=pl.DeviceIdType.MESH,
         )
 
-    start_buf[chip * n_sub + sub] = start_ref[...].T
-    for copy in tile_copies:
+    for copy in small_copies + tile_copies:
         copy.wait()
     for block in range(n_col):
         for column in range(local_cols):
@@ -244,7 +270,7 @@
     for step in range(1, devices):
         peer = lax.rem(me + step, devices)
         push(remote(sums_buf, me, sums_send.at[step], sums_recv.at[me], device_place(peer)))
-    for step in range(1, chips):
+    for step in range(chips - 1, 0, -1):
         peer = lax.rem(chip + step, chips)
         index = peer * n_sub + sub
         remote(
@@ -296,7 +322,7 @@
 
     def orthonormalize(inverse):
         for p in range(pieces):
-            current_ref[p] = full_dot(inverse, residual_ref[p])
+            current_ref[p] = plain_dot(inverse, residual_ref[p])
 
     own_lanes = pl.ds(pl.multiple_of(col * half, half), half)
     own_piece = row * n_sub + sub
@@ -353,7 +379,7 @@
             for p in range(pieces):
                 previous_ref[p] = current_ref[p]
         orthonormalize(inverse)
-        for step in range(1, n_row):
+        for step in range(n_row - 1, 0, -1):
             peer = lax.rem(row + step, n_row)
             index = peer * n_sub + sub
             remote(
@@ -379,28 +405,62 @@
         alpha = jnp.zeros((width, width), jnp.float32)
         for p in range(pieces):
             if iteration > 0:
-                mixed = full_dot(
+                mixed = plain_dot(
                     jnp.concatenate([inverse, -upper], axis=1),
                     jnp.concatenate([got[p], previous_ref[p]], axis=0),
                 )
             else:
-                mixed = full_dot(inverse, got[p])
+                mixed = plain_dot(inverse, got[p])
             residual_ref[p] = mixed
             alpha = alpha + dot_last(current_ref[p], mixed)
         alphas_ref[iteration] = alpha
         turned = alpha.T
         for p in range(pieces):
-            residual_ref[p] = residual_ref[p] - full_dot(turned, current_ref[p])
+            residual_ref[p] = residual_ref[p] - plain_dot(turned, current_ref[p])
 
     _, inverse = factorize_residual(alphas_ref.shape[0])
     rows_own = pl.ds(pl.multiple_of(sub * half_width, half_width), half_width)
     mine_buf[...] = inverse
     for s in range(n_sub):
-        panel_ref[s * half : (s + 1) * half, :] = full_dot(
+        panel_ref[:, s * half : (s + 1) * half] = plain_dot(
             mine_buf[rows_own, :], residual_ref[row * n_sub + s, :, own_lanes]
-        ).T
+        )
     for copy in sent:
         copy.wait_send()
+
+
+def hand_out_kernel(*refs):
+    count = len(refs) // 3
+    sources, targets, held = refs[:count], refs[count : 2 * count], refs[2 * count : 3 * count]
+    sem = refs[-1]
+    inward = [
+        pltpu.make_async_copy(source, here, sem.at[0, at])
+        for at, (source, here) in enumerate(zip(sources, held))
+    ]
+    outward = [
+        pltpu.make_async_copy(here, target, sem.at[1, at])
+        for at, (here, target) in enumerate(zip(held, targets))
+    ]
+    for copy in inward:
+        copy.start()
+    for copy, onward in zip(inward, outward):
+        copy.wait()
+        onward.start()
+    for copy in outward:
+        copy.wait()
+
+
+def hand_out(*arrays):
+    in_hbm = pl.BlockSpec(memory_space=pltpu.HBM)
+    return pl.pallas_call(
+        hand_out_kernel,
+        out_shape=tuple(jax.ShapeDtypeStruct(array.shape, array.dtype) for array in arrays),
+        in_specs=[in_hbm] * len(arrays),
+        out_specs=(in_hbm,) * len(arrays),
+        scratch_shapes=[pltpu.VMEM(array.shape, array.dtype) for array in arrays]
+        + [pltpu.SemaphoreType.DMA((2, len(arrays)))],
+        compiler_params=pltpu.CompilerParams(vmem_limit_bytes=60 * 2**20),
+    )(*arrays)
 
 
 def dense_on_device(tiles, tile_rows, tile_cols, tile_counts, start_panel):
@@ -414,19 +474,22 @@
     pieces = n_row * n_sub
     span = n_col * half
     in_vmem = pl.BlockSpec(memory_space=pltpu.VMEM)
-    in_smem = pl.BlockSpec(memory_space=pltpu.SMEM)
     f32 = jnp.float32
     dma = pltpu.SemaphoreType.DMA
-    return pl.pallas_call(
+    panel, alphas, betas = pl.pallas_call(
         functools.partial(lanczos_kernel, n_row, n_col, n_sub),
         out_shape=(
-            jax.ShapeDtypeStruct(start_panel.shape, f32),
+            jax.ShapeDtypeStruct((half_width, side), f32),
             jax.ShapeDtypeStruct((ITERS, width, width), f32),
             jax.ShapeDtypeStruct((ITERS + 1, width, width), f32),
         ),
-        in_specs=[in_smem, in_smem, in_smem, pl.BlockSpec(memory_space=pl.ANY), in_vmem],
+        in_specs=[pl.BlockSpec(memory_space=pltpu.HBM)] * 5,
         out_specs=(in_vmem, in_vmem, in_vmem),
         scratch_shapes=[
+            pltpu.SMEM(tile_rows.shape, jnp.int32),
+            pltpu.SMEM(tile_cols.shape, jnp.int32),
+            pltpu.SMEM(tile_counts.shape, jnp.int32),
+            dma((4,)),
             pltpu.VMEM((slots, half, side), f32),
             pltpu.VMEM((span, slots // n_col * side), jnp.bfloat16),
             pltpu.VMEM((span, slots // n_col * side), jnp.bfloat16),
@@ -454,9 +517,11 @@
             dma((ITERS, n_row, n_sub)),
         ],
         compiler_params=pltpu.CompilerParams(
-            collective_id=0, has_side_effects=True, vmem_limit_bytes=40 * 2**20
+            collective_id=0, has_side_effects=True, vmem_limit_bytes=60 * 2**20
         ),
-    )(tile_rows, tile_cols, tile_counts, tiles, start_panel)
+    )(tile_rows, tile_cols, tile_counts, tiles, start_panel.T)
+    panel, alphas, betas = hand_out(panel, alphas, betas)
+    return panel.T, alphas, betas
 
 
 def on_one_device(tiles, tile_rows, tile_cols, tile_counts, start_panel):

time: 53.6 us -> 47.2 us (0.88)
  local copies, waits for them, and re-layouts: 5.64 us -> 0 us
  Pallas kernels: 46.4 us -> 45.7 us
    unnamed x9 -> x0, local copies, waits for them, and re-layouts: 4.96 us -> none
    pallas_call x1, Pallas kernels: 46.4 us -> 44.1 us  [dense_on_device(): pl.pallas_call(functools.partial(lanczos_kernel, n_row, n_col, n_sub), ou...]
    pallas_call x0 -> x1, Pallas kernels: none -> 1.57 us  [hand_out(): pl.pallas_call(hand_out_kernel, out_shape=tuple((jax.ShapeDtypeStruct(arr...]
    pallas_call x1 -> x0, local copies, waits for them, and re-layouts: 0.68 us -> none  [dense_on_device(): pl.pallas_call(functools.partial(lanczos_kernel, n_row, n_col, n_sub), ou...]
where the time goes in v4:
time: 47.2 us; the launch traced here: 47 us
  Pallas kernels  45.7 us (97%)
  between operations  1.29 us (3%)
    pallas_call x1, Pallas kernels, dense_on_device(): pl.pallas_call(functools.partial(lanczos_kernel, n_row, n_col, n_sub), ou...  44.1 us
    pallas_call x1, Pallas kernels, hand_out(): pl.pallas_call(hand_out_kernel, out_shape=tuple((jax.ShapeDtypeStruct(arr...  1.57 us

profile of v4, /device:TPU:1, one launch (start us, length us, event | category | flops | bytes accessed | tf_op | source)
XLA Modules:
  0.0 47.0 jit_solution(8078440297503067070)
XLA Ops:
  1.3 44.1 %shard_map.76 = (f32[16,256]{1,0:T(8,128)}, f32[3,32,32]{2,1,0:T(8,128)}, f32[4,32,32]{2,1,0:T(8,128)}) custom-call(s32[8]{0:T(128)} %rows_any.1, s32[8]{0:T(128)} %cols_any.1, s32[1]{0:T(128)S(6)} %copy.8.count_any, f32[8,256,256]{2,1,0:T(8,128)} %tiles_ref.1, f32[16,256]{1,0:T(8,128)} %bitcast.2), custom_call_target="tpu_custom_call" | custom-call | tf_op jit(solution)/shard_map/pallas_call | solution.py:479
  45.4 1.6 %shard_map.77 = (f32[16,256]{1,0:T(8,128)}, f32[3,32,32]{2,1,0:T(8,128)}, f32[4,32,32]{2,1,0:T(8,128)}) custom-call(f32[16,256]{1,0:T(8,128)} %get-tuple-element.9.refs_0_, f32[3,32,32]{2,1,0:T(8,128)} %get-tuple-element.10.refs_1_, f32[4,32,32]{2,1,0:T(8,128)} %get-tuple-element.11.refs_2_), custom_call_target="tpu_custom_call" | custom-call | tf_op jit(solution)/shard_map/pallas_call | solution.py:455
